TPU v7x, 128 devices: a whole 4x4x4 slice. The times are simulated.
128 devices in a mesh: tok: 64 (over x, y, z), grp: 2 (over core).
Axes of the slice: x: 4, y: 4, z: 4, core: 2. Of those that a mesh axis runs over, the one named last changes fastest.
Arguments:
- tokens: bfloat16 [131072, 1536], P('tok', 'grp'), may hold values from -8 to 8
- slot_keys: bfloat16 [1536, 256], P('tok', 'grp'), may hold values from -2 to 2
- w_in: bfloat16 [2, 64, 1536, 1024], P('grp', 'tok'), may hold values from -0.3125 to 0.3125
- w_out: bfloat16 [2, 64, 1024, 1536], P('grp', 'tok'), may hold values from -0.1875 to 0.1875
- out_grad: bfloat16 [131072, 1536], P('tok', 'grp'), may hold values from -0.59765625 to 0.59765625
Outputs:
- layer_out: bfloat16 [131072, 1536], P('tok', 'grp')
- tokens_grad: bfloat16 [131072, 1536], P('tok', 'grp')
- keys_grad: float32 [1536, 256], P('tok', 'grp')
- w_in_grad: bfloat16 [2, 64, 1536, 1024], P('grp', 'tok')
- w_out_grad: bfloat16 [2, 64, 1024, 1536], P('grp', 'tok')
All inputs are finite; a program needn't handle non-finite values.
Results may differ from a plain program's by a relative error of at most 0.02.
Values may be sent and summed in bfloat16 or wider, within the bound.
A program may use at most 192 MiB of HBM per device.

v0:
```python
import math

import jax
import jax.numpy as jnp
from jax import lax
from jax.sharding import PartitionSpec as P

SLOTS_EXP = 2


def gelu_exact(argument):
    return 0.5 * argument * (1.0 + jax.scipy.special.erf(argument / math.sqrt(2.0)))


def gelu_slope(argument):
    cumulative = 0.5 * (1.0 + jax.scipy.special.erf(argument / math.sqrt(2.0)))
    density = jnp.exp(-0.5 * argument * argument) / math.sqrt(2.0 * math.pi)
    return cumulative + argument * density


def contract_rows(former, latter):
    return lax.dot_general(
        former, latter, (((0,), (0,)), ((), ())), preferred_element_type=jnp.float32
    )


def contract_cols(former, latter):
    return lax.dot_general(
        former, latter, (((1,), (1,)), ((), ())), preferred_element_type=jnp.float32
    )


def column_softmax(logits):
    local_top = jnp.max(logits, axis=0)
    col_peak = lax.pmax(local_top, "tok")
    weights = jnp.exp(logits - col_peak[None, :])
    col_total = lax.psum(jnp.sum(weights, axis=0), "tok")
    return (weights, col_total)


def row_softmax(logits):
    local_top = jnp.max(logits, axis=1)
    row_peak = lax.pmax(local_top, "grp")
    weights = jnp.exp(logits - row_peak[:, None])
    row_total = lax.psum(jnp.sum(weights, axis=1), "grp")
    return (weights, row_total)


def body(tokens, slot_keys, w_in, w_out, out_grad):
    tok_index = lax.axis_index("tok")
    features, grad_rows = (
        lax.all_gather(tokens, "grp", axis=1, tiled=True),
        lax.all_gather(out_grad, "grp", axis=1, tiled=True),
    )
    key_cols = lax.all_gather(slot_keys, "tok", axis=0, tiled=True)
    logits = jnp.dot(features, key_cols, preferred_element_type=jnp.float32)
    disp_exp, disp_total = column_softmax(logits)
    disp_weight = disp_exp.astype(jnp.bfloat16)
    columns = disp_weight
    slot_part = lax.psum_scatter(
        contract_rows(columns, features), "tok", scatter_dimension=0, tiled=True
    )
    own_total = lax.dynamic_slice_in_dim(disp_total, tok_index * SLOTS_EXP, SLOTS_EXP, 0)
    slot_in_f = slot_part / own_total[:, None]
    slot_in = slot_in_f.astype(jnp.bfloat16)
    in_matrix = w_in[0, 0]
    out_matrix = w_out[0, 0]
    pre_act = jnp.dot(slot_in, in_matrix, preferred_element_type=jnp.float32)
    hidden = gelu_exact(pre_act).astype(jnp.bfloat16)
    slot_out = jnp.dot(hidden, out_matrix, preferred_element_type=jnp.float32).astype(jnp.bfloat16)
    slot_all = lax.all_gather(slot_out, "tok", axis=0, tiled=True)
    comb_exp, comb_total = row_softmax(logits)
    comb_weight = comb_exp.astype(jnp.bfloat16)
    partial_value = jnp.dot(comb_weight, slot_all, preferred_element_type=jnp.float32)
    layer_sum = lax.psum_scatter(
        partial_value.astype(jnp.bfloat16), "grp", scatter_dimension=1, tiled=True
    ).astype(jnp.float32)
    layer_out = (layer_sum / comb_total[:, None]).astype(jnp.bfloat16)
    scaled_grad = (grad_rows / comb_total[:, None]).astype(jnp.bfloat16)
    columns = comb_weight
    out_slot_grad = lax.psum_scatter(
        contract_rows(columns, scaled_grad), "tok", scatter_dimension=0, tiled=True
    ).astype(jnp.bfloat16)
    w_out_grad = contract_rows(hidden, out_slot_grad).astype(jnp.bfloat16)
    hidden_grad = contract_cols(out_slot_grad, out_matrix)
    pre_grad = (hidden_grad * gelu_slope(pre_act)).astype(jnp.bfloat16)
    w_in_grad = contract_rows(slot_in, pre_grad).astype(jnp.bfloat16)
    slot_in_grad = contract_cols(pre_grad, in_matrix)
    routed = (slot_in_grad / own_total[:, None]).astype(jnp.bfloat16)
    out_dot = contract_cols(grad_rows, slot_all)
    mix_part = jnp.sum(comb_exp * out_dot, axis=1)
    mix_dot = lax.psum(mix_part, "grp") / comb_total
    routed_all = lax.all_gather(routed, "tok", axis=0, tiled=True)
    in_dot = contract_cols(features, routed_all)
    disp_part = jnp.sum(disp_exp * in_dot, axis=0)
    disp_dot = lax.psum(disp_part, "tok") / disp_total
    logit_grad = (
        comb_exp / comb_total[:, None] * (out_dot - mix_dot[:, None])
        + disp_exp * (in_dot - disp_dot[None, :])
    ).astype(jnp.bfloat16)
    both_weight = jnp.concatenate([disp_weight, logit_grad], axis=1)
    both_values = jnp.concatenate([routed_all, key_cols.T], axis=0)
    token_part = jnp.dot(both_weight, both_values, preferred_element_type=jnp.float32)
    token_sum = lax.psum_scatter(
        token_part.astype(jnp.bfloat16), "grp", scatter_dimension=1, tiled=True
    )
    columns = features
    keys_grad = lax.psum_scatter(
        contract_rows(columns, logit_grad), "tok", scatter_dimension=0, tiled=True
    )
    return (
        layer_out,
        token_sum,
        keys_grad,
        w_in_grad.reshape(w_in.shape),
        w_out_grad.reshape(w_out.shape),
    )


def solution(mesh):
    placed = (
        P("tok", "grp"),
        P("tok", "grp"),
        P("grp", "tok", None, None),
        P("grp", "tok", None, None),
        P("tok", "grp"),
    )
    return jax.shard_map(
        body,
        mesh=mesh,
        in_specs=placed,
        out_specs=(
            P("tok", "grp"),
            P("tok", "grp"),
            P("tok", "grp"),
            P("grp", "tok", None, None),
            P("grp", "tok", None, None),
        ),
        check_vma=False,
    )
```

profile of v0, /device:TPU:1, one launch (start us, length us, event | category | flops | bytes accessed | tf_op | source)
XLA Modules:
  0.0 1653.7 jit_solution(8982197239417088659)
XLA Ops:
  7.2 0.0 copy-start
  7.2 0.0 all-gather.5.cloned.1.call-start
  7.2 0.7 all-gather.5.cloned.1.call-update
  7.9 0.0 all-reduce.8.cloned.1.call-start
  8.0 153.4 %all_gather.16 = bf16[1536,128]{1,0:T(8,128)(2,1)S(1)} all-gather(bf16[24,128]{1,0:T(8,128)(2,1)} %param.6), channel_id=1, replica_groups=mesh['tok'=64,'grp'=2] {'tok'}, dimensions={0}, use_global_device_ids=true | all-gather | bytes 399360 | tf_op jit(solution)/shard_map/all_gather | solution.py:55
  161.3 0.0 all-gather.5.cloned.1.call-done
  161.3 6.0 fusion.53
  167.3 144.2 %pmax.15 = f32[128]{0:T(128)S(1)} all-reduce(f32[128]{0:T(128)S(1)} %get-tuple-element.22), channel_id=1, replica_groups=mesh['tok'=64,'grp'=2] {'tok'}, use_global_device_ids=true, to_apply=%region_3.0 | all-reduce | flops 128 | bytes 1024 | tf_op jit(solution)/shard_map/pmax | solution.py:35
  311.5 0.0 copy-start.6
  311.5 1.6 fusion.52
  313.1 0.0 copy-start.1
  313.1 0.8 copy-done.1
  313.9 4.7 fusion.54
  318.6 0.0 copy-done.6
  318.6 0.0 all-reduce.8.cloned.1.call-update
  318.6 0.0 all-gather.7.cloned.1.call-start
  318.6 0.7 all-gather.7.cloned.1.call-update
  319.3 0.0 all-reduce.10.cloned.1.call-start
  319.4 1.3 dynamic-slice
  321.3 145.3 %psum.28 = f32[128]{0:T(128)S(1)} all-reduce(f32[128]{0:T(128)S(1)} %get-tuple-element.18), channel_id=1, replica_groups=mesh['tok'=64,'grp'=2] {'tok'}, use_global_device_ids=true, to_apply=%region_6.0 | all-reduce | flops 128 | bytes 1024 | tf_op jit(solution)/shard_map/psum | solution.py:37
  466.6 0.6 dynamic_slice.3
  467.2 0.0 copy-done.8
  467.3 86.5 %pmax.14 = f32[2048]{0:T(1024)S(1)} all-reduce(f32[2048]{0:T(1024)S(1)} %get-tuple-element.17), channel_id=1, replica_groups=mesh['tok'=64,'grp'=2] {'grp'}, use_global_device_ids=true, to_apply=%region_1.0 | all-reduce | flops 2048 | bytes 16384 | tf_op jit(solution)/shard_map/pmax | solution.py:43
  553.8 2.5 fusion.9
  556.3 0.0 copy-done
  556.3 0.5 fusion.20
  556.8 153.4 %all-gather = bf16[64,2,1536]{2,1,0:T(2,128)(2,1)} all-gather(bf16[1,2,1536]{2,1,0:T(2,128)(2,1)S(1)} %fusion.20), channel_id=1, replica_groups=mesh['tok'=64,'grp'=2] {'tok'}, dimensions={0}, use_global_device_ids=true | all-gather | bytes 399360 | tf_op jit(solution)/shard_map/all_gather | solution.py:71
  710.2 1.9 reshape.25
  712.1 6.9 multiply_reduce_fusion.1
  719.0 32.5 %all-reduce.3 = (f32[2048]{0:T(1024)}, f32[2048]{0:T(1024)}) all-reduce(f32[2048]{0:T(1024)} %get-tuple-element.16, f32[2048]{0:T(1024)} %get-tuple-element.15), channel_id=1, replica_groups=mesh['tok'=64,'grp'=2] {'grp'}, use_global_device_ids=true, to_apply=%region_9.0 | all-reduce | flops 4096 | bytes 32768 | tf_op jit(solution)/shard_map/psum | solution.py:45
  751.5 1.3 div.61
  752.8 5.4 fusion
  758.2 295.4 %all-reduce.11 = bf16[128,1536]{1,0:T(8,128)(2,1)} all-reduce(f32[128,1536]{1,0:T(8,128)} %fusion), channel_id=4, replica_groups=mesh['tok'=64,'grp'=2] {'tok'}, use_global_device_ids=true, to_apply=%region_12.0.clone | all-reduce | flops 196608 | bytes 1179648
  1053.6 1.6 fusion.29
  1055.3 0.6 copy-done.4
  1055.9 2.8 fusion.23
  1058.7 153.8 %all-gather.1 = bf16[64,2,1536]{2,1,0:T(2,128)(2,1)} all-gather(bf16[1,2,1536]{2,1,0:T(2,128)(2,1)S(1)} %fusion.23), channel_id=1, replica_groups=mesh['tok'=64,'grp'=2] {'tok'}, dimensions={0}, use_global_device_ids=true | all-gather | bytes 399360 | tf_op jit(solution)/shard_map/all_gather | solution.py:93
  1212.5 1.9 reshape.27
  1214.4 6.8 multiply_reduce_fusion
  1221.2 146.7 %psum.31 = f32[128]{0:T(128)} all-reduce(f32[128]{0:T(128)} %get-tuple-element.25), channel_id=1, replica_groups=mesh['tok'=64,'grp'=2] {'tok'}, use_global_device_ids=true, to_apply=%region_14.0 | all-reduce | flops 128 | bytes 1024 | tf_op jit(solution)/shard_map/psum | solution.py:96
  1367.9 0.7 div.67
  1368.6 2.3 add_convert_fusion
  1370.9 0.0 copy-start.2
  1370.9 0.8 copy-done.2
  1371.7 4.7 convolution_bitcast_fusion.2
  1376.4 0.0 all-reduce.10.cloned.1.call-update
  1376.4 0.2 reduce-scatter.4.cloned.1.call-start
  1376.6 5.8 convolution_convert_fusion.1
  1382.4 0.0 reduce-scatter.4.cloned.1.call-update
  1382.5 0.0 reduce-scatter.6.cloned.1.call-start
  1382.5 1.9 copy.12
  1384.4 5.8 convolution_convert_fusion
  1390.3 0.0 reduce-scatter.6.cloned.1.call-update
  1390.9 0.0 copy-done.5
  1390.9 0.0 copy-done.7
  1390.9 3.6 fusion.1
  1394.5 3.4 fusion.2
  1397.9 208.1 %all-reduce.10.cloned.1.call-done = f32[1536,128]{0,1:T(8,128)} async-done(((f32[1536,128]{0,1:T(8,128)}), f32[1536,128]{0,1:T(8,128)}) %all-reduce.10.cloned.1.call-update) | async-done | bytes 786448
  1606.1 1.0 constant_dynamic-slice_fusion
  1607.0 0.7 copy.13
  1607.7 17.6 %reduce-scatter.4.cloned.1.call-done = bf16[2048,768]{1,0:T(8,128)(2,1)} async-done(((bf16[2048,1536]{1,0:T(8,128)(2,1)}), bf16[2048,768]{1,0:T(8,128)(2,1)}) %reduce-scatter.4.cloned.1.call-update) | async-done | bytes 3145744 | tf_op jit(solution)/shard_map/reduce_scatter | solution.py:75
  1625.3 0.0 copy-done.3
  1625.3 4.2 divide_convert_fusion.1
  1629.5 17.3 %reduce-scatter.6.cloned.1.call-done = bf16[2048,768]{1,0:T(8,128)(2,1)} async-done(((bf16[2048,1536]{1,0:T(8,128)(2,1)}), bf16[2048,768]{1,0:T(8,128)(2,1)}) %reduce-scatter.6.cloned.1.call-update) | async-done | bytes 3145744 | tf_op jit(solution)/shard_map/reduce_scatter | solution.py:104
  (7 shorter events, 0.0 us)
Async XLA Ops:
  7.2 549.1 %copy-start = (bf16[1,1,1024,1536]{3,2,1,0:T(8,128)(2,1)S(1)}, bf16[1,1,1024,1536]{3,2,1,0:T(8,128)(2,1)}, u32[]{:S(2)}) copy-start(bf16[1,1,1024,1536]{3,2,1,0:T(8,128)(2,1)} %param.8) | copy-start | bytes 9437188
  7.2 154.1 %all-gather.5.cloned.1.call-start = ((), (), s32[]{:S(2)}) async-start(), calls=%async_computation.2 | async-start | bytes 9437184 | tf_op jit(solution)/shard_map/all_gather | solution.py:52
  7.9 545.9 %all-reduce.8.cloned.1.call-start = ((), (), s32[]{:S(2)}) async-start(), calls=%async_computation.6 | async-start | bytes 1572864
  311.5 7.0 copy-start.6
  313.1 0.8 copy-start.1
  318.6 393.6 %all-gather.7.cloned.1.call-start = ((), (), s32[]{:S(2)}) async-start(), calls=%async_computation.4 | async-start | bytes 9437184 | tf_op jit(solution)/shard_map/all_gather | solution.py:53
  319.3 1286.7 %all-reduce.10.cloned.1.call-start = ((), (), s32[]{:S(2)}) async-start(), calls=%async_computation.7 | async-start | bytes 1572864
  466.6 0.6 copy-start.8
  1055.3 0.6 copy-start.4
  1370.9 0.8 copy-start.2
  1376.4 248.9 %reduce-scatter.4.cloned.1.call-start = ((), (), s32[]{:S(2)}) async-start(), calls=%async_computation.3 | async-start | bytes 9437184 | tf_op jit(solution)/shard_map/reduce_scatter | solution.py:75
  1382.5 264.4 %reduce-scatter.6.cloned.1.call-start = ((), (), s32[]{:S(2)}) async-start(), calls=%async_computation.5 | async-start | bytes 9437184 | tf_op jit(solution)/shard_map/reduce_scatter | solution.py:104
  1384.4 6.5 copy-start.5
  1384.4 6.5 copy-start.7
  1390.3 235.1 %copy-start.3 = (f32[2048]{0:T(1024)S(1)}, f32[2048]{0:T(1024)}, u32[]{:S(2)}) copy-start(f32[2048]{0:T(1024)} %get-tuple-element.19) | copy-start | bytes 24580
Sparse Core Ops, SparseCore 0:
  9.7 23.0 all-gather.4
  318.7 177.3 all-reduce.7
  497.8 19.1 all-gather.6
  1376.5 229.4 all-reduce.9
  1608.3 16.9 reduce-scatter.3
  1628.3 18.4 reduce-scatter.5
where the time goes:
time: 1650 us
  blocking collectives  1310 us (79%)
  waiting for transfers between devices  244 us (15%)
  matrix products  60.4 us (4%)
    unnamed x1, blocking collectives  295 us
    unnamed x8, waiting for transfers between devices  210 us
    all_gather x1, blocking collectives, body(): routed_all = lax.all_gather(routed, 'tok', axis=0, tiled=True)  154 us
    all_gather x1, blocking collectives, body(): slot_all = lax.all_gather(slot_out, 'tok', axis=0, tiled=True)  153 us
    all_gather x1, blocking collectives, body(): key_cols = lax.all_gather(slot_keys, 'tok', axis=0, tiled=True)  153 us
    psum x1, blocking collectives, body(): disp_dot = lax.psum(disp_part, 'tok') / disp_total  147 us
    psum x1, blocking collectives, column_softmax(): col_total = lax.psum(jnp.sum(weights, axis=0), 'tok')  145 us
    pmax x1, blocking collectives, column_softmax(): col_peak = lax.pmax(local_top, 'tok')  144 us
  transfers between devices with their start and end apart: 6, of which 3 were waited for; matrix products, arithmetic and copies ran while one was open for 2% of the time, Pallas kernels for 0%

commit v1 on v0

v1 whole, which is shorter than its diff:
```python
import functools
import math

import jax
import jax.numpy as jnp
from jax import lax
from jax.experimental import pallas as pl
from jax.experimental.pallas import tpu as pltpu
from jax.sharding import PartitionSpec as P

MESH = pl.DeviceIdType.MESH
F32 = jnp.float32
BF16 = jnp.bfloat16

NT = 64
SIDE = 4
TOK = 2048
HALF = 768
WIDTH = 1536
HID = 1024
SLOTS = 256
SLOT_ROWS = 4
GROUPS6 = HALF // 128
DATA_ROWS = SLOT_ROWS * GROUPS6
MSG_ROWS = 32
CHUNK = 512
NCHUNK = TOK // CHUNK
KROWS = 24

CONTRACT_ROWS = (((0,), (0,)), ((), ()))
CONTRACT_COLS = (((1,), (1,)), ((), ()))


def dot_nn(a, b):
    return jnp.dot(a, b, preferred_element_type=F32)


def dot_tn(a, b):
    return lax.dot_general(a, b, CONTRACT_ROWS, preferred_element_type=F32)


def dot_nt(a, b):
    return lax.dot_general(a, b, CONTRACT_COLS, preferred_element_type=F32)


def gelu_parts(v):
    cumulative = 0.5 * (1.0 + lax.erf(v * (1.0 / math.sqrt(2.0))))
    density = jnp.exp(-0.5 * v * v) * (1.0 / math.sqrt(2.0 * math.pi))
    return v * cumulative, cumulative + v * density


def rows_at(c):
    return pl.ds(pl.multiple_of(c * CHUNK, CHUNK), CHUNK)


def split_hi_lo(value, shape):
    lane = lax.broadcasted_iota(jnp.int32, shape, 1)
    hi = value.astype(BF16).astype(F32)
    return jnp.where(lane < 64, hi, value - hi)


def join_hi_lo(value):
    return value + pltpu.roll(value, 64, 1)


def kernel(
    tokens, keys, w_in, w_out, grads,
    lay_out, tok_out, key_out, win_out, wout_out,
    x, dy, wi, wo, part, logit, comb, combw, dispw, lgs, lgr, lg, lay, tgr, wig, wog,
    acc, flat, keyf, keymsg, keyland, osgmsg, osgland, slotmsg, slotland, outmsg, outland,
    rtmsg, rtland, kgmsg, kgland, sval, rval, colmax, colsum,
    osgx, slotx, outx, outr, rtx, rtr, arow, grow, srow, prow,
    load_sem, out_sem, pair_s, pair_r, ls, lr, gs, gr, a2a_s, a2a_r,
):
    t = lax.axis_index("tok")
    g = lax.axis_index("grp")
    other = 1 - g
    cx, cy, cz = t // 16, lax.rem(t // 4, 4), lax.rem(t, 4)

    loads = [
        pltpu.make_async_copy(tokens, x, load_sem.at[0]),
        pltpu.make_async_copy(grads, dy, load_sem.at[1]),
        pltpu.make_async_copy(w_out.at[0, 0], wo, load_sem.at[2]),
        pltpu.make_async_copy(w_in.at[0, 0], wi, load_sem.at[3]),
    ]
    for copy in loads:
        copy.start()

    barrier = pltpu.get_barrier_semaphore()

    def greet(i, _):
        p = lax.rem(t + i, NT)
        pl.semaphore_signal(barrier, inc=1, device_id={"tok": p, "grp": g}, device_id_type=MESH)
        pl.semaphore_signal(barrier, inc=1, device_id={"tok": p, "grp": other}, device_id_type=MESH)
        return 0

    lax.fori_loop(1, NT, greet, 0)
    pl.semaphore_signal(barrier, inc=1, device_id={"tok": t, "grp": other}, device_id_type=MESH)

    row = lax.broadcasted_iota(jnp.int32, (128, 128), 0)
    col = lax.broadcasted_iota(jnp.int32, (128, 128), 1)
    order = jnp.where(row == 2 * lax.rem(col, 64) + col // 64, 1.0, 0.0).astype(BF16)
    keymsg[0:KROWS, :] = dot_nn(keys[...], order).astype(BF16)
    pl.semaphore_wait(barrier, 2 * NT - 1)

    def partner(i):
        a, b, c = i // 16, lax.rem(i // 4, 4), lax.rem(i, 4)
        px, py, pz = lax.rem(cx + 6 - a, 4), lax.rem(cy + 6 - b, 4), lax.rem(cz + 6 - c, 4)
        return px * 16 + py * 4 + pz

    def each_partner(send):
        def step(i, _):
            send(partner(i))
            return 0

        lax.fori_loop(0, 42, step, 0)
        lax.fori_loop(43, NT, step, 0)

    def pair_copy(i, src, dst):
        return pltpu.make_async_remote_copy(
            src, dst, pair_s.at[i], pair_r.at[i], device_id={"tok": t, "grp": other}, device_id_type=MESH
        )

    def landed(i, buffer):
        pltpu.make_async_copy(buffer, buffer, a2a_r.at[i]).wait()

    def sent(i, block):
        pltpu.make_async_copy(block, block, a2a_s.at[i]).wait()

    half = t // 32
    place = g * 32 + lax.rem(t, 32)

    def send_keys(p):
        pltpu.make_async_remote_copy(
            keymsg, keyland.at[place], a2a_s.at[0], a2a_r.at[0],
            device_id={"tok": p, "grp": half}, device_id_type=MESH,
        ).start()

    each_partner(send_keys)

    @pl.when(half == g)
    def _():
        pltpu.make_async_copy(keymsg, keyland.at[place], a2a_r.at[0]).start()

    @pl.when(half != g)
    def _():
        pltpu.make_async_remote_copy(
            keymsg, keyland.at[place], a2a_s.at[0], a2a_r.at[0],
            device_id={"tok": t, "grp": other}, device_id_type=MESH,
        ).start()

    landed(0, keyland)
    for h in range(2):
        block = keyland[h * 32:(h + 1) * 32, 0:KROWS, :].astype(F32)
        keyf[:, h * 128:(h + 1) * 128] = block.reshape(HALF, 128).astype(BF16)

    def logit_copy(c):
        return pltpu.make_async_remote_copy(
            part.at[rows_at(c)], logit.at[rows_at(c)], ls.at[c], lr.at[c],
            device_id={"tok": t, "grp": other}, device_id_type=MESH,
        )

    loads[0].wait()

    def logits_step(c, _):
        part[rows_at(c), :] = dot_nn(x[rows_at(c), :], keyf[...])
        logit_copy(c).start()
        return 0

    lax.fori_loop(0, NCHUNK, logits_step, 0)

    loads[1].wait()
    colmax[...] = jnp.full((8, SLOTS), -jnp.inf, F32)
    acc[...] = jnp.zeros((SLOTS, HALF), F32)

    def comb_step(c, _):
        rows = rows_at(c)
        logit_copy(c).wait_recv()
        values = logit[rows, :] + part[rows, :]
        logit[rows, :] = values
        colmax[...] = jnp.maximum(colmax[...], jnp.max(values.reshape(CHUNK // 8, 8, SLOTS), axis=0))
        weights = jnp.exp(values - jnp.max(values, axis=1, keepdims=True))
        weights = weights / jnp.sum(weights, axis=1, keepdims=True)
        comb[rows, :] = weights
        low = weights.astype(BF16)
        combw[rows, :] = low
        acc[...] += dot_tn(low, dy[rows, :])
        return 0

    lax.fori_loop(0, NCHUNK, comb_step, 0)

    def to_messages():
        for j in range(SLOT_ROWS):
            for q in range(GROUPS6):
                flat[pl.ds(4 * q + j, NT, stride=MSG_ROWS), :] = acc[64 * j:64 * (j + 1), 128 * q:128 * (q + 1)]

    def from_messages(dst):
        for j in range(SLOT_ROWS):
            for q in range(GROUPS6):
                dst[64 * j:64 * (j + 1), 128 * q:128 * (q + 1)] = (
                    flat[pl.ds(4 * q + j, NT, stride=MSG_ROWS), :].astype(BF16)
                )

    def to_lanes(r):
        column = jnp.concatenate(
            [flat[pl.ds(r + j, NT, stride=MSG_ROWS), :] for j in range(SLOT_ROWS)], axis=0
        )
        return column.T[0:1, :]

    def scatter(i, msg, land):
        def send(p):
            pltpu.make_async_remote_copy(
                msg.at[p], land.at[t], a2a_s.at[i], a2a_r.at[i],
                device_id={"tok": p, "grp": g}, device_id_type=MESH,
            ).start()

        each_partner(send)
        pltpu.make_async_copy(msg.at[t], land.at[t], a2a_r.at[i]).start()

    def spread(i, msg, land):
        def send(p):
            pltpu.make_async_remote_copy(
                msg, land.at[t], a2a_s.at[i], a2a_r.at[i],
                device_id={"tok": p, "grp": g}, device_id_type=MESH,
            ).start()

        each_partner(send)
        pltpu.make_async_copy(msg, land.at[t], a2a_r.at[i]).start()

    to_messages()
    osgmsg[...] = flat[...].reshape(NT, MSG_ROWS, 128).astype(BF16)
    scatter(1, osgmsg, osgland)

    peak = jnp.max(colmax[...], axis=0, keepdims=True).astype(BF16).astype(F32)
    acc[...] = jnp.zeros((SLOTS, HALF), F32)
    colsum[...] = jnp.zeros((8, SLOTS), F32)

    def disp_step(c, _):
        rows = rows_at(c)
        weights = jnp.exp(logit[rows, :] - peak)
        colsum[...] += jnp.sum(weights.reshape(CHUNK // 8, 8, SLOTS), axis=0)
        acc[...] += dot_tn(weights.astype(BF16), x[rows, :])
        return 0

    lax.fori_loop(0, NCHUNK, disp_step, 0)
    total = jnp.sum(colsum[...], axis=0, keepdims=True)
    peak_col = jnp.broadcast_to(peak, (128, SLOTS)).T
    total_col = split_hi_lo(jnp.broadcast_to(total, (128, SLOTS)).T, (SLOTS, 128))
    to_messages()
    for j in range(SLOT_ROWS):
        flat[pl.ds(DATA_ROWS + j, NT, stride=MSG_ROWS), :] = peak_col[64 * j:64 * (j + 1), :]
        flat[pl.ds(DATA_ROWS + 4 + j, NT, stride=MSG_ROWS), :] = total_col[64 * j:64 * (j + 1), :]
    slotmsg[...] = flat[...].reshape(NT, MSG_ROWS, 128).astype(BF16)
    scatter(2, slotmsg, slotland)

    row16 = lax.broadcasted_iota(jnp.int32, (16, 1), 0)
    mine = jnp.where(row16 // 2 == g, 1.0, 0.0).astype(F32)

    def to_rows(dst, src):
        dst[...] = jnp.zeros((16, WIDTH), F32)
        for h in range(2):
            for q in range(GROUPS6):
                at = (h * GROUPS6 + q) * 128
                dst[0:SLOT_ROWS, at:at + 128] = src[h, 4 * q:4 * q + 4, :]

    def from_rows(dst, value):
        for h in range(2):
            for q in range(GROUPS6):
                at = (h * GROUPS6 + q) * 128
                dst[h, 4 * q:4 * q + 4, :] = value[0:SLOT_ROWS, at:at + 128]

    landed(1, osgland)
    osgx[g, :, :] = jnp.sum(osgland[:, 0:DATA_ROWS, :].astype(F32), axis=0)
    osg_pair = pair_copy(0, osgx.at[g], osgx.at[g])
    osg_pair.start()
    osg_pair.wait_recv()
    to_rows(grow, osgx)
    out_grad = (grow[...] * mine).astype(BF16)
    loads[2].wait()
    hidden_grad = dot_nt(out_grad, wo[...])

    landed(2, slotland)
    stats = slotland[:, DATA_ROWS:MSG_ROWS, :].astype(F32)
    row8 = lax.broadcasted_iota(jnp.int32, (NT, 8, 128), 1)
    swapped = jnp.concatenate([stats[:, 4:8, :], stats[:, 0:4, :]], axis=1)
    peaks = jnp.where(row8 < 4, stats, swapped)
    totals = jnp.where(row8 < 4, swapped, stats)
    top = jnp.max(peaks, axis=0)
    scale = jnp.exp(peaks - top[None])
    whole = join_hi_lo(jnp.sum(scale * totals, axis=0))
    for q in range(DATA_ROWS // 8):
        block = slotland[:, 8 * q:8 * (q + 1), :].astype(F32)
        slotx[g, 8 * q:8 * (q + 1), :] = jnp.sum(block * scale, axis=0) / whole
    slot_pair = pair_copy(1, slotx.at[g], slotx.at[g])
    slot_pair.start()
    slot_pair.wait_recv()
    to_rows(srow, slotx)
    slot_in = srow[...].astype(BF16)
    loads[3].wait()
    pre_act = dot_nn(slot_in, wi[...])
    hidden, slope = gelu_parts(pre_act)
    hidden = hidden.astype(BF16)
    slot_out = dot_nn(hidden, wo[...]) * mine
    from_rows(outx, slot_out)
    out_pair = pair_copy(2, outx.at[other], outr)
    out_pair.start()
    out_pair.wait_recv()
    outmsg[0:DATA_ROWS, :] = (outx[g, :, :] + outr[...]).astype(BF16)
    spread(3, outmsg, outland)

    pre_grad = (hidden_grad * slope).astype(BF16)
    slot_in_grad = dot_nt(pre_grad, wi[...])
    arow[...] = jnp.zeros((16, 128), F32)
    arow[0:SLOT_ROWS, :] = whole[0:SLOT_ROWS, :]
    whole_rows = jnp.where(row16 < SLOT_ROWS, arow[...], 1.0)
    routed = slot_in_grad / jnp.concatenate([whole_rows] * (WIDTH // 128), axis=1)
    routed = routed.astype(BF16).astype(F32) * mine
    from_rows(rtx, routed)
    products = srow[...] * routed
    for h in range(2):
        share = jnp.sum(products[:, h * HALF:(h + 1) * HALF], axis=1, keepdims=True)
        share = jnp.broadcast_to(share, (16, 128))
        rtx[h, DATA_ROWS:DATA_ROWS + 4, :] = top[0:SLOT_ROWS, :] * mine[0:SLOT_ROWS, :]
        rtx[h, DATA_ROWS + 4:MSG_ROWS, :] = share[0:SLOT_ROWS, :]
    rt_pair = pair_copy(3, rtx.at[other], rtr)
    rt_pair.start()
    rt_pair.wait_recv()
    rtmsg[0:DATA_ROWS, :] = (rtx[g, 0:DATA_ROWS, :] + rtr[0:DATA_ROWS, :]).astype(BF16)
    tail = rtx[g, DATA_ROWS:MSG_ROWS, :] + rtr[DATA_ROWS:MSG_ROWS, :]
    lane8 = lax.broadcasted_iota(jnp.int32, (8, 128), 1)
    row8b = lax.broadcasted_iota(jnp.int32, (8, 128), 0)
    high = tail.astype(BF16).astype(F32)
    tail = jnp.where((row8b < 4) | (lane8 < 64), high, tail - high)
    rtmsg[DATA_ROWS:MSG_ROWS, :] = tail.astype(BF16)
    spread(4, rtmsg, rtland)

    wog[...] = dot_tn(hidden, out_grad).astype(BF16)
    wout_copy = pltpu.make_async_copy(wog, wout_out.at[0, 0], out_sem.at[0])
    wout_copy.start()
    wig[...] = dot_tn(slot_in, pre_grad).astype(BF16)
    win_copy = pltpu.make_async_copy(wig, win_out.at[0, 0], out_sem.at[1])
    win_copy.start()

    landed(3, outland)
    flat[...] = outland[...].astype(F32).reshape(NT * MSG_ROWS, 128)
    from_messages(sval)

    def out_step(c, _):
        rows = rows_at(c)
        lay[rows, :] = dot_nn(combw[rows, :], sval[...]).astype(BF16)
        pltpu.make_async_copy(lay.at[rows], lay_out.at[rows], out_sem.at[2]).start()
        weights = comb[rows, :]
        out_dot = dot_nt(dy[rows, :], sval[...])
        mix = jnp.sum(weights * out_dot, axis=1, keepdims=True)
        comb[rows, :] = weights * (out_dot - mix)
        return 0

    lax.fori_loop(0, NCHUNK, out_step, 0)

    landed(4, rtland)
    flat[...] = rtland[...].astype(F32).reshape(NT * MSG_ROWS, 128)
    from_messages(rval)
    top_row = to_lanes(DATA_ROWS)
    lane_sum = jnp.concatenate(
        [flat[pl.ds(DATA_ROWS + 4 + j, NT, stride=MSG_ROWS), :] for j in range(SLOT_ROWS)], axis=0
    )
    disp_dot = join_hi_lo(lane_sum).T[0:1, :]

    def grad_copy(c):
        return pltpu.make_async_remote_copy(
            lgs.at[rows_at(c)], lgr.at[rows_at(c)], gs.at[c], gr.at[c],
            device_id={"tok": t, "grp": other}, device_id_type=MESH,
        )

    def in_step(c, _):
        rows = rows_at(c)
        weights = jnp.exp(logit[rows, :] - top_row)
        dispw[rows, :] = weights.astype(BF16)
        in_dot = dot_nt(x[rows, :], rval[...])
        lgs[rows, :] = (comb[rows, :] + weights * (in_dot - disp_dot)).astype(BF16)
        grad_copy(c).start()
        return 0

    lax.fori_loop(0, NCHUNK, in_step, 0)
    acc[...] = jnp.zeros((SLOTS, HALF), F32)

    def keys_step(c, _):
        rows = rows_at(c)
        grad_copy(c).wait_recv()
        low = (lgs[rows, :].astype(F32) + lgr[rows, :].astype(F32)).astype(BF16)
        lg[rows, :] = low
        acc[...] += dot_tn(low, x[rows, :])
        return 0

    lax.fori_loop(0, NCHUNK, keys_step, 0)

    for h in range(2):
        for q in range(GROUPS6):
            turned = acc[h * 128:(h + 1) * 128, q * 128:(q + 1) * 128].T
            flat[h * HALF + q * 128:h * HALF + (q + 1) * 128, :] = turned
    kgmsg[:, 0:KROWS, :] = flat[0:2 * HALF, :].reshape(NT, KROWS, 128).astype(BF16)

    def key_target(i):
        a, b, c, d = i // 32, lax.rem(i // 8, 4), lax.rem(i // 2, 4), lax.rem(i, 2)
        py, pz = lax.rem(cy + 6 - b, 4), lax.rem(cz + 6 - c, 4)
        return a * 16 + py * 4 + pz, d

    def send_grad(i, _):
        p, d = key_target(i)

        @pl.when((g * 32 + p != t) | (d != g))
        def _():
            pltpu.make_async_remote_copy(
                kgmsg.at[d * 32 + p], kgland.at[t], a2a_s.at[5], a2a_r.at[5],
                device_id={"tok": g * 32 + p, "grp": d}, device_id_type=MESH,
            ).start()

        return 0

    lax.fori_loop(0, NT, send_grad, 0)

    @pl.when(half == g)
    def _():
        pltpu.make_async_copy(kgmsg.at[g * 32 + lax.rem(t, 32)], kgland.at[t], a2a_r.at[5]).start()

    def tok_step(c, _):
        rows = rows_at(c)
        value = dot_nn(dispw[rows, :], rval[...]) + dot_nt(lg[rows, :], keyf[...])
        tgr[rows, :] = value.astype(BF16)
        pltpu.make_async_copy(tgr.at[rows], tok_out.at[rows], out_sem.at[3]).start()
        return 0

    lax.fori_loop(0, NCHUNK, tok_step, 0)

    landed(5, kgland)
    key_out[...] = jnp.sum(kgland[:, 0:KROWS, :].astype(F32), axis=0)

    for pair in (osg_pair, slot_pair, out_pair, rt_pair):
        pair.wait_send()

    def drain(c, _):
        logit_copy(c).wait_send()
        grad_copy(c).wait_send()
        return 0

    lax.fori_loop(0, NCHUNK, drain, 0)
    sent(1, osgmsg.at[pl.ds(0, NT - 1)])
    sent(2, slotmsg.at[pl.ds(0, NT - 1)])
    sent(3, outland.at[pl.ds(0, NT - 1)])
    sent(4, rtland.at[pl.ds(0, NT - 1)])

    @pl.when(half == g)
    def _():
        sent(0, keyland.at[pl.ds(0, NT - 1)])
        sent(5, kgmsg.at[pl.ds(0, NT - 1)])

    @pl.when(half != g)
    def _():
        sent(0, keyland)
        sent(5, kgmsg)

    wout_copy.wait()
    win_copy.wait()
    pltpu.make_async_copy(lay, lay_out, out_sem.at[2]).wait()
    pltpu.make_async_copy(tgr, tok_out, out_sem.at[3]).wait()


def body(tokens, slot_keys, w_in, w_out, out_grad):
    anywhere = pl.BlockSpec(memory_space=pl.ANY)
    vmem = pl.BlockSpec(memory_space=pltpu.VMEM)
    buf = pltpu.VMEM
    dma = pltpu.SemaphoreType.DMA
    messages = buf((NT, MSG_ROWS, 128), BF16)
    layer_out, tokens_grad, keys_grad, w_in_grad, w_out_grad = pl.pallas_call(
        kernel,
        out_shape=(
            jax.ShapeDtypeStruct((TOK, HALF), BF16),
            jax.ShapeDtypeStruct((TOK, HALF), BF16),
            jax.ShapeDtypeStruct((KROWS, 128), F32),
            jax.ShapeDtypeStruct(w_in.shape, BF16),
            jax.ShapeDtypeStruct(w_out.shape, BF16),
        ),
        in_specs=[anywhere, vmem, anywhere, anywhere, anywhere],
        out_specs=[anywhere, anywhere, vmem, anywhere, anywhere],
        scratch_shapes=[
            buf((TOK, HALF), BF16),
            buf((TOK, HALF), BF16),
            buf((WIDTH, HID), BF16),
            buf((HID, WIDTH), BF16),
            buf((TOK, SLOTS), F32),
            buf((TOK, SLOTS), F32),
            buf((TOK, SLOTS), F32),
            buf((TOK, SLOTS), BF16),
            buf((TOK, SLOTS), BF16),
            buf((TOK, SLOTS), BF16),
            buf((TOK, SLOTS), BF16),
            buf((TOK, SLOTS), BF16),
            buf((TOK, HALF), BF16),
            buf((TOK, HALF), BF16),
            buf((WIDTH, HID), BF16),
            buf((HID, WIDTH), BF16),
            buf((SLOTS, HALF), F32),
            buf((NT * MSG_ROWS, 128), F32),
            buf((HALF, SLOTS), BF16),
            buf((MSG_ROWS, 128), BF16),
            messages,
            messages,
            messages,
            messages,
            messages,
            buf((MSG_ROWS, 128), BF16),
            messages,
            buf((MSG_ROWS, 128), BF16),
            messages,
            messages,
            messages,
            buf((SLOTS, HALF), BF16),
            buf((SLOTS, HALF), BF16),
            buf((8, SLOTS), F32),
            buf((8, SLOTS), F32),
            buf((2, DATA_ROWS, 128), F32),
            buf((2, DATA_ROWS, 128), F32),
            buf((2, DATA_ROWS, 128), F32),
            buf((DATA_ROWS, 128), F32),
            buf((2, MSG_ROWS, 128), F32),
            buf((MSG_ROWS, 128), F32),
            buf((16, 128), F32),
            buf((16, WIDTH), F32),
            buf((16, WIDTH), F32),
            buf((16, WIDTH), F32),
            dma((4,)),
            dma((4,)),
            dma((4,)),
            dma((4,)),
            dma((NCHUNK,)),
            dma((NCHUNK,)),
            dma((NCHUNK,)),
            dma((NCHUNK,)),
            dma((6,)),
            dma((6,)),
        ],
        compiler_params=pltpu.CompilerParams(
            collective_id=0, has_side_effects=True, vmem_limit_bytes=60 * 1024 * 1024
        ),
        name="moe",
    )(tokens, slot_keys, w_in, w_out, out_grad)
    keys_grad = keys_grad.reshape(KROWS, 2, 64).transpose(0, 2, 1).reshape(KROWS, 128)
    return layer_out, tokens_grad, keys_grad, w_in_grad, w_out_grad


def solution(mesh):
    placed = (
        P("tok", "grp"),
        P("tok", "grp"),
        P("grp", "tok", None, None),
        P("grp", "tok", None, None),
        P("tok", "grp"),
    )
    return jax.shard_map(
        body,
        mesh=mesh,
        in_specs=placed,
        out_specs=(
            P("tok", "grp"),
            P("tok", "grp"),
            P("tok", "grp"),
            P("grp", "tok", None, None),
            P("grp", "tok", None, None),
        ),
        check_vma=False,
    )
```

time: 1650 us -> 90.8 us (0.06)
  blocking collectives: 1310 us -> 0 us
  waiting for transfers between devices: 244 us -> 0 us
  Pallas kernels: 0 us -> 76.7 us
  matrix products: 60.4 us -> 0 us
    all_gather x3 -> x0, blocking collectives: 461 us -> none  [the longest x1 154 us: body(): routed_all = lax.all_gather(routed, 'tok', axis=0, tiled=True)]
    psum x3 -> x0, blocking collectives: 325 us -> none  [the longest x1 147 us: body(): disp_dot = lax.psum(disp_part, 'tok') / disp_total]
    unnamed x1 -> x0, blocking collectives: 295 us -> none
    pmax x2 -> x0, blocking collectives: 231 us -> none  [the longest x1 144 us: column_softmax(): col_peak = lax.pmax(local_top, 'tok')]
    unnamed x8 -> x0, waiting for transfers between devices: 210 us -> none
    pallas_call x0 -> x1, Pallas kernels: none -> 76.7 us  [body(): pl.pallas_call(kernel, out_shape=(jax.ShapeDtypeStruct((TOK, HALF), BF16)...]
    dot_general x14 -> x0, matrix products: 60.4 us -> none  [the longest x5 21.7 us: contract_rows(): lax.dot_general(former, latter, (((0,), (0,)), ((), ())), preferred_eleme...]
    reduce_scatter x2 -> x0, waiting for transfers between devices: 34.9 us -> none  [the longest x1 17.6 us: body(): lax.psum_scatter(partial_value.astype(jnp.bfloat16), 'grp', scatter_dimen...]
  transfers between devices with their start and end apart: 6 -> 0, of which waited for: 3 -> 0; matrix products, arithmetic and copies ran while one was open for 2% -> 0% of each run, Pallas kernels for 0% -> 0%
where the time goes in v1:
time: 90.8 us; the launch traced here: 90.6 us
  Pallas kernels  76.7 us (84%)
  local copies, waits for them, and re-layouts  13.2 us (15%)
    pallas_call x1, Pallas kernels, body(): pl.pallas_call(kernel, out_shape=(jax.ShapeDtypeStruct((TOK, HALF), BF16)...  76.7 us
    unnamed x11, local copies, waits for them, and re-layouts  12.3 us

profile of v1, /device:TPU:1, one launch (start us, length us, event | category | flops | bytes accessed | tf_op | source)
XLA Modules:
  0.0 90.6 jit_solution(2747377888929409535)
XLA Ops:
  0.6 76.7 %moe.1 = (bf16[2048,768]{1,0:T(8,128)(2,1)}, bf16[2048,768]{1,0:T(8,128)(2,1)}, f32[24,128]{1,0:T(8,128)}, bf16[1,1,1536,1024]{3,2,1,0:T(8,128)(2,1)}, bf16[1,1,1024,1536]{3,2,1,0:T(8,128)(2,1)}) custom-call(bf16[2048,768]{1,0:T(8,128)(2,1)} %tokens.1, bf16[24,128]{1,0:T(8,128)(2,1)} %keys.1, bf16[1,1,1536,1024]{3,2,1,0:T(8,128)(2,1)} %w_in.1, ...), custom_call_target="tpu_custom_call" | custom-call | tf_op jit(solution)/shard_map/moe/pallas_call | solution.py:474
  77.4 0.8 reshape.16
  78.2 0.1 copy.11
  78.3 0.7 copy.12
  78.9 0.0 copy-start.2
  78.9 3.9 %copy.17 = bf16[2048,768]{1,0:T(8,128)(2,1)} copy(bf16[2048,768]{1,0:T(8,128)(2,1)} %get-tuple-element.25) | data formatting | bytes 6291456
  82.8 0.0 copy-done.2
  82.8 0.0 copy-start.1
  82.9 1.7 %copy.18 = bf16[2048,768]{1,0:T(8,128)(2,1)} copy(bf16[2048,768]{1,0:T(8,128)(2,1)S(1)} %copy-done.2) | data formatting | bytes 6291456
  84.5 1.4 %copy-done.1 = bf16[1,1,1536,1024]{3,2,1,0:T(8,128)(2,1)S(1)} copy-done((bf16[1,1,1536,1024]{3,2,1,0:T(8,128)(2,1)S(1)}, bf16[1,1,1536,1024]{3,2,1,0:T(8,128)(2,1)}, u32[]{:S(2)}) %copy-start.1) | copy-done | bytes 3145752
  85.9 0.0 copy-start
  85.9 1.7 %copy.19 = bf16[1,1,1536,1024]{3,2,1,0:T(8,128)(2,1)} copy(bf16[1,1,1536,1024]{3,2,1,0:T(8,128)(2,1)S(1)} %copy-done.1) | data formatting | bytes 6291456
  87.5 1.4 %copy-done = bf16[1,1,1024,1536]{3,2,1,0:T(8,128)(2,1)S(1)} copy-done((bf16[1,1,1024,1536]{3,2,1,0:T(8,128)(2,1)S(1)}, bf16[1,1,1024,1536]{3,2,1,0:T(8,128)(2,1)}, u32[]{:S(2)}) %copy-start) | copy-done | bytes 3145752
  88.9 1.7 %copy.20 = bf16[1,1,1024,1536]{3,2,1,0:T(8,128)(2,1)} copy(bf16[1,1,1024,1536]{3,2,1,0:T(8,128)(2,1)S(1)} %copy-done) | data formatting | bytes 6291456
Async XLA Ops:
  78.9 3.9 %copy-start.2 = (bf16[2048,768]{1,0:T(8,128)(2,1)S(1)}, bf16[2048,768]{1,0:T(8,128)(2,1)}, u32[]{:S(2)}) copy-start(bf16[2048,768]{1,0:T(8,128)(2,1)} %get-tuple-element.26) | copy-start | bytes 9437188
  82.8 3.0 %copy-start.1 = (bf16[1,1,1536,1024]{3,2,1,0:T(8,128)(2,1)S(1)}, bf16[1,1,1536,1024]{3,2,1,0:T(8,128)(2,1)}, u32[]{:S(2)}) copy-start(bf16[1,1,1536,1024]{3,2,1,0:T(8,128)(2,1)} %get-tuple-element.28) | copy-start | bytes 9437188
  85.9 3.0 %copy-start = (bf16[1,1,1024,1536]{3,2,1,0:T(8,128)(2,1)S(1)}, bf16[1,1,1024,1536]{3,2,1,0:T(8,128)(2,1)}, u32[]{:S(2)}) copy-start(bf16[1,1,1024,1536]{3,2,1,0:T(8,128)(2,1)} %get-tuple-element.29) | copy-start | bytes 9437188

commit v2 on v1

v2 whole, which is shorter than its diff:
```python
import functools
import math

import jax
import jax.numpy as jnp
from jax import lax
from jax.experimental import pallas as pl
from jax.experimental.pallas import tpu as pltpu
from jax.sharding import PartitionSpec as P

MESH = pl.DeviceIdType.MESH
F32 = jnp.float32
BF16 = jnp.bfloat16

NT = 64
SIDE = 4
TOK = 2048
HALF = 768
WIDTH = 1536
HID = 1024
SLOTS = 256
SLOT_ROWS = 4
GROUPS6 = HALF // 128
DATA_ROWS = SLOT_ROWS * GROUPS6
CHUNK = 512
NCHUNK = TOK // CHUNK
KROWS = 24
PIECES = 4
LOWEST = -1e38

CONTRACT_ROWS = (((0,), (0,)), ((), ()))
CONTRACT_COLS = (((1,), (1,)), ((), ()))


def dot_nn(a, b):
    return jnp.dot(a, b, preferred_element_type=F32)


def dot_tn(a, b):
    return lax.dot_general(a, b, CONTRACT_ROWS, preferred_element_type=F32)


def dot_nt(a, b):
    return lax.dot_general(a, b, CONTRACT_COLS, preferred_element_type=F32)


def gelu_parts(v):
    cumulative = 0.5 * (1.0 + lax.erf(v * (1.0 / math.sqrt(2.0))))
    density = jnp.exp(-0.5 * v * v) * (1.0 / math.sqrt(2.0 * math.pi))
    return v * cumulative, cumulative + v * density


def rows_at(c):
    if isinstance(c, int):
        return pl.ds(c * CHUNK, CHUNK)
    return pl.ds(pl.multiple_of(c * CHUNK, CHUNK), CHUNK)


def each_chunk(step):
    lax.fori_loop(0, NCHUNK, lambda c, _: (step(c), 0)[1], 0)


def split_hi_lo(value, shape):
    lane = lax.broadcasted_iota(jnp.int32, shape, 1)
    hi = value.astype(BF16).astype(F32)
    return jnp.where(lane < 64, hi, value - hi)


def join_hi_lo(value):
    return value + pltpu.roll(value, 64, 1)


def kernel(
    tokens, keys, w_in, w_out, grads,
    lay_out, tok_out, key_out, win_out, wout_out,
    x, dy, wi, wo, wit, wot, part, logit, comb, combw, dispw, lgs, lgr, lg,
    acc, acc2, flat, keyf, keyown, keymsg, keyland, osgmsg, osgland, slotmsg, slotland, outmsg, outland,
    rtmsg, rtland, kgmsg, kgland, sval, rval, colmax, colsum,
    osgx, osgown, osgboth, slotx, outx, outr, rtx, arow, grow, srow,
    load_sem, out_sem, pair_s, pair_r, ls, lr, gs, gr, a2a_s, a2a_r,
):
    t = lax.axis_index("tok")
    g = lax.axis_index("grp")
    other = 1 - g
    cx, cy, cz = t // 16, lax.rem(t // 4, 4), lax.rem(t, 4)

    loads = [
        pltpu.make_async_copy(keys, keyown, load_sem.at[4]),
        pltpu.make_async_copy(tokens, x, load_sem.at[0]),
        pltpu.make_async_copy(grads, dy, load_sem.at[1]),
        pltpu.make_async_copy(w_out.at[0, 0], wo, load_sem.at[2]),
        pltpu.make_async_copy(w_in.at[0, 0], wi, load_sem.at[3]),
    ]
    for copy in loads:
        copy.start()

    barrier = pltpu.get_barrier_semaphore()

    def partner(i):
        a, b, c = i // 16, lax.rem(i // 4, 4), lax.rem(i, 4)
        px, py, pz = lax.rem(cx + 6 - a, 4), lax.rem(cy + 6 - b, 4), lax.rem(cz + 6 - c, 4)
        return px * 16 + py * 4 + pz

    def each_partner(send):
        def step(i, _):
            send(partner(i))
            return 0

        lax.fori_loop(0, 42, step, 0, unroll=True)
        lax.fori_loop(43, NT, step, 0, unroll=True)

    def greet(p):
        pl.semaphore_signal(barrier, inc=1, device_id={"tok": p, "grp": g}, device_id_type=MESH)
        pl.semaphore_signal(barrier, inc=1, device_id={"tok": p, "grp": other}, device_id_type=MESH)

    each_partner(greet)
    pl.semaphore_signal(barrier, inc=1, device_id={"tok": t, "grp": other}, device_id_type=MESH)

    row = lax.broadcasted_iota(jnp.int32, (128, 128), 0)
    col = lax.broadcasted_iota(jnp.int32, (128, 128), 1)
    loads[0].wait()
    order = jnp.where(row == 2 * lax.rem(col, 64) + col // 64, 1.0, 0.0).astype(BF16)
    keymsg[...] = dot_nn(keyown[...], order).astype(BF16)
    pl.semaphore_wait(barrier, 2 * NT - 1)

    def pair_copy(i, src, dst):
        return pltpu.make_async_remote_copy(
            src, dst, pair_s.at[i], pair_r.at[i], device_id={"tok": t, "grp": other}, device_id_type=MESH
        )

    def landed(i, buffer):
        pltpu.make_async_copy(buffer, buffer, a2a_r.at[i]).wait()

    def sent(i, block):
        pltpu.make_async_copy(block, block, a2a_s.at[i]).wait()

    half = t // 32
    place = g * 32 + lax.rem(t, 32)

    def send_keys(p):
        pltpu.make_async_remote_copy(
            keymsg, keyland.at[place], a2a_s.at[0], a2a_r.at[0],
            device_id={"tok": p, "grp": half}, device_id_type=MESH,
        ).start()

    each_partner(send_keys)

    @pl.when(half == g)
    def _():
        pltpu.make_async_copy(keymsg, keyland.at[place], a2a_r.at[0]).start()

    @pl.when(half != g)
    def _():
        pltpu.make_async_remote_copy(
            keymsg, keyland.at[place], a2a_s.at[0], a2a_r.at[0],
            device_id={"tok": t, "grp": other}, device_id_type=MESH,
        ).start()

    loads[3].wait()

    def turn_out(i, _):
        at = pl.ds(pl.multiple_of(i * 256, 256), 256)
        wot[:, at] = wo[at, :].T
        return 0

    lax.fori_loop(0, HID // 256, turn_out, 0)
    loads[4].wait()

    def turn_in(i, _):
        at = pl.ds(pl.multiple_of(i * 256, 256), 256)
        wit[:, at] = wi[at, :].T
        return 0

    lax.fori_loop(0, WIDTH // 256, turn_in, 0)

    landed(0, keyland)
    for h in range(2):
        block = keyland[h * 32:(h + 1) * 32, :, :].astype(F32)
        keyf[:, h * 128:(h + 1) * 128] = block.reshape(HALF, 128).astype(BF16)

    def logit_copy(c, group):
        lanes = pl.ds(128 * group, 128)
        return pltpu.make_async_remote_copy(
            part.at[rows_at(c), lanes], logit.at[rows_at(c), lanes],
            ls.at[group, c], lr.at[group, c],
            device_id={"tok": t, "grp": other}, device_id_type=MESH,
        )

    loads[1].wait()

    def logits_step(c):
        part[rows_at(c), :] = dot_nn(x[rows_at(c), :], keyf[...])
        logit_copy(c, 0).start()

    each_chunk(logits_step)
    each_chunk(lambda c: logit_copy(c, 1).start())

    for group in range(2):
        lanes = slice(128 * group, 128 * (group + 1))
        colmax[...] = jnp.full((8, 128), LOWEST, F32)
        colsum[...] = jnp.zeros((8, 128), F32)
        acc2[...] = jnp.zeros((128, HALF), F32)

        def disp_step(c):
            rows = rows_at(c)
            logit_copy(c, group).wait_recv()
            values = logit[rows, lanes] + part[rows, lanes]
            logit[rows, lanes] = values
            peak = jnp.max(jnp.max(values.reshape(CHUNK // 8, 8, 128), axis=0), axis=0, keepdims=True)
            peak = jnp.maximum(peak, colmax[0:1, :]).astype(BF16).astype(F32)
            weights = jnp.exp(values - peak)
            sums = jnp.sum(weights.reshape(CHUNK // 8, 8, 128), axis=0)
            rows_sum = dot_tn(weights.astype(BF16), x[rows, :])
            shift = jnp.exp(colmax[0:1, :] - peak)
            shift_col = jnp.broadcast_to(shift, (128, 128)).T
            for q in range(GROUPS6):
                at = slice(128 * q, 128 * (q + 1))
                acc2[:, at] = acc2[:, at] * shift_col + rows_sum[:, at]
            colsum[...] = colsum[...] * shift + sums
            colmax[0:1, :] = peak

        each_chunk(disp_step)

        peak_col = jnp.broadcast_to(colmax[0:1, :], (128, 128)).T
        total = jnp.sum(colsum[...], axis=0, keepdims=True)
        total_col = split_hi_lo(jnp.broadcast_to(total, (128, 128)).T, (128, 128))
        stat = jnp.where(g == 0, peak_col, total_col)
        for j in range(2):
            for q in range(GROUPS6):
                flat[pl.ds(2 * q + j, NT, stride=24), :] = acc2[64 * j:64 * (j + 1), 128 * q:128 * (q + 1)]
            flat[pl.ds(12 + j, NT, stride=24), :] = stat[64 * j:64 * (j + 1), :]
            flat[pl.ds(14 + j, NT, stride=24), :] = stat[64 * j:64 * (j + 1), :]
        slotmsg[group, :, :, :] = flat[0:NT * 24, :].reshape(NT, 24, 128)[:, 0:16, :].astype(BF16)

        def send_slots(p, group=group):
            pltpu.make_async_remote_copy(
                slotmsg.at[group, p], slotland.at[g, t], a2a_s.at[2], a2a_r.at[2],
                device_id={"tok": p, "grp": group}, device_id_type=MESH,
            ).start()

        each_partner(send_slots)

        @pl.when(g == group)
        def _():
            pltpu.make_async_copy(slotmsg.at[group, t], slotland.at[g, t], a2a_r.at[2]).start()

        @pl.when(g != group)
        def _():
            send_slots(t)

    def from_messages(dst, land):
        flat[0:NT * DATA_ROWS, :] = land[...].astype(F32).reshape(NT * DATA_ROWS, 128)
        for j in range(SLOT_ROWS):
            for q in range(GROUPS6):
                r = (j // 2) * 12 + 2 * q + j % 2
                dst[64 * j:64 * (j + 1), 128 * q:128 * (q + 1)] = (
                    flat[pl.ds(r, NT, stride=DATA_ROWS), :].astype(BF16)
                )

    def scatter(i, msg, land):
        def send(p):
            pltpu.make_async_remote_copy(
                msg.at[p], land.at[t], a2a_s.at[i], a2a_r.at[i],
                device_id={"tok": p, "grp": g}, device_id_type=MESH,
            ).start()

        each_partner(send)
        pltpu.make_async_copy(msg.at[t], land.at[t], a2a_r.at[i]).start()

    def spread(i, msg, land):
        def send(p):
            pltpu.make_async_remote_copy(
                msg, land.at[t], a2a_s.at[i], a2a_r.at[i],
                device_id={"tok": p, "grp": g}, device_id_type=MESH,
            ).start()

        each_partner(send)
        pltpu.make_async_copy(msg, land.at[t], a2a_r.at[i]).start()

    loads[2].wait()
    def comb_step(c):
        rows = rows_at(c)
        values = logit[rows, :]
        weights = jnp.exp(values - jnp.max(values, axis=1, keepdims=True))
        weights = weights / jnp.sum(weights, axis=1, keepdims=True)
        comb[rows, :] = weights
        combw[rows, :] = weights.astype(BF16)

    each_chunk(comb_step)
    acc[...] = jnp.zeros((SLOTS, HALF), F32)

    def slot_grad_step(c):
        acc[...] += dot_tn(combw[rows_at(c), :], dy[rows_at(c), :])

    each_chunk(slot_grad_step)
    osgown[...] = acc[...].astype(BF16)
    osg_pair = pair_copy(0, osgown.at[pl.ds(pl.multiple_of(other * 128, 128), 128)], osgboth.at[g])
    osg_pair.start()
    osgboth[g, :, :] = osgown[pl.ds(pl.multiple_of(g * 128, 128), 128), :]
    osg_pair.wait_recv()
    for h in range(2):
        for j in range(2):
            for q in range(GROUPS6):
                value = osgboth[h, 64 * j:64 * (j + 1), 128 * q:128 * (q + 1)]
                flat[pl.ds((h * GROUPS6 + q) * 2 + j, NT, stride=DATA_ROWS), :] = value.astype(F32)
    osgmsg[...] = flat[0:NT * DATA_ROWS, :].reshape(NT, DATA_ROWS, 128).astype(BF16)
    scatter(1, osgmsg, osgland)

    row16 = lax.broadcasted_iota(jnp.int32, (16, 1), 0)

    def to_rows(dst, block_of):
        dst[...] = jnp.zeros((16, WIDTH), F32)
        for at in range(WIDTH // 128):
            dst[0:2, 128 * at:128 * (at + 1)] = block_of(at)

    landed(2, slotland)
    tail0 = slotland[0, :, 8:16, :].astype(F32)
    tail1 = slotland[1, :, 8:16, :].astype(F32)
    row8 = lax.broadcasted_iota(jnp.int32, (NT, 8, 128), 1)
    swapped = jnp.concatenate([tail0[:, 4:8, :], tail0[:, 0:4, :]], axis=1)
    peaks = jnp.where(row8 < 4, swapped, tail0)
    top = jnp.max(peaks, axis=0)
    scale = jnp.exp(peaks - top[None])
    whole = join_hi_lo(jnp.sum(scale * tail1, axis=0))
    whole = jnp.concatenate([whole[4:8, :], whole[4:8, :]], axis=0)
    for h, tail in ((0, tail0), (1, tail1)):
        head = slotland[h, :, 0:8, :].astype(F32)
        slotx[h, 0:8, :] = jnp.sum(head * scale, axis=0) / whole
        slotx[h, 8:16, :] = jnp.sum(tail * scale, axis=0) / whole
    to_rows(srow, lambda at: slotx[at // GROUPS6, 2 * (at % GROUPS6):2 * (at % GROUPS6) + 2, :])
    slot_in = srow[...].astype(BF16)
    pre_act = dot_nn(slot_in, wi[...])
    hidden, slope = gelu_parts(pre_act)
    hidden = hidden.astype(BF16)
    slot_out = dot_nn(hidden, wo[...])
    for at in range(WIDTH // 128):
        h, q = at // GROUPS6, at % GROUPS6
        outx[h, 2 * q:2 * q + 2, :] = slot_out[0:2, 128 * at:128 * (at + 1)]
    out_pair = pair_copy(2, outx.at[other], outr.at[g])
    out_pair.start()
    outr[g, :, :] = outx[g, :, :]
    out_pair.wait_recv()
    outmsg[...] = jnp.concatenate([outr[0, 0:12, :], outr[1, 0:12, :]], axis=0).astype(BF16)
    spread(3, outmsg, outland)

    landed(1, osgland)
    osgx[...] = jnp.sum(osgland[...].astype(F32), axis=0)
    to_rows(grow, lambda at: osgx[2 * at:2 * at + 2, :])
    out_grad = grow[...].astype(BF16)
    hidden_grad = dot_nn(out_grad, wot[...])
    pre_grad = (hidden_grad * slope).astype(BF16)
    slot_in_grad = dot_nn(pre_grad, wit[...])
    arow[...] = jnp.zeros((16, 128), F32)
    arow[0:2, :] = whole[0:2, :]
    top_own = top[0:2, :]
    whole_rows = jnp.where(row16 < 2, arow[...], 1.0)
    routed = slot_in_grad / jnp.concatenate([whole_rows] * (WIDTH // 128), axis=1)
    routed = routed.astype(BF16).astype(F32)
    products = srow[...] * routed
    lane4 = lax.broadcasted_iota(jnp.int32, (2, 128), 1)
    for h in range(2):
        share = jnp.sum(products[:, h * HALF:(h + 1) * HALF], axis=1, keepdims=True)
        own = [routed[0:2, :], top_own, share[0:2, :]]
        for q in range(GROUPS6):
            at = (h * GROUPS6 + q) * 128
            rtx[h, 2 * q:2 * q + 2, :] = own[0][:, at:at + 128]
        rtx[h, 12:14, :] = own[1]
        value = jnp.broadcast_to(own[2], (2, 128))
        high = value.astype(BF16).astype(F32)
        rtx[h, 14:16, :] = jnp.where(lane4 < 64, high, value - high)
    rtmsg[...] = rtx[...].astype(BF16)

    def send_routed(p):
        for h, core in ((0, 0), (1, 1)):
            pltpu.make_async_remote_copy(
                rtmsg.at[h], rtland.at[g, t], a2a_s.at[4], a2a_r.at[4],
                device_id={"tok": p, "grp": core}, device_id_type=MESH,
            ).start()

    each_partner(send_routed)
    pltpu.make_async_remote_copy(
        rtmsg.at[other], rtland.at[g, t], a2a_s.at[4], a2a_r.at[4],
        device_id={"tok": t, "grp": other}, device_id_type=MESH,
    ).start()
    pltpu.make_async_copy(rtmsg.at[g], rtland.at[g, t], a2a_r.at[4]).start()

    wout_out[0, 0] = dot_tn(hidden, out_grad).astype(BF16)
    win_out[0, 0] = dot_tn(slot_in, pre_grad).astype(BF16)

    landed(3, outland)
    from_messages(sval, outland)

    def out_step(c):
        rows = rows_at(c)
        lay_out[rows, :] = dot_nn(combw[rows, :], sval[...]).astype(BF16)
        weights = comb[rows, :]
        out_dot = dot_nt(dy[rows, :], sval[...])
        mix = jnp.sum(weights * out_dot, axis=1, keepdims=True)
        comb[rows, :] = weights * (out_dot - mix)

    each_chunk(out_step)

    landed(4, rtland)
    flat[0:2 * NT * 16, :] = rtland[...].astype(F32).reshape(2 * NT * 16, 128)

    def routed_rows(j, r):
        return flat[pl.ds((j // 2) * NT * 16 + r + j % 2, NT, stride=16), :]

    for j in range(SLOT_ROWS):
        for q in range(GROUPS6):
            rval[64 * j:64 * (j + 1), 128 * q:128 * (q + 1)] = routed_rows(j, 2 * q).astype(BF16)
    top_row = jnp.concatenate([routed_rows(j, 12) for j in range(SLOT_ROWS)], axis=0).T[0:1, :]
    lane_sum = jnp.concatenate([routed_rows(j, 14) for j in range(SLOT_ROWS)], axis=0)
    disp_dot = join_hi_lo(lane_sum).T[0:1, :]

    def grad_copy(c):
        return pltpu.make_async_remote_copy(
            lgs.at[rows_at(c)], lgr.at[rows_at(c)], gs.at[c], gr.at[c],
            device_id={"tok": t, "grp": other}, device_id_type=MESH,
        )

    def in_step(c):
        rows = rows_at(c)
        weights = jnp.exp(logit[rows, :] - top_row)
        dispw[rows, :] = weights.astype(BF16)
        in_dot = dot_nt(x[rows, :], rval[...])
        lgs[rows, :] = (comb[rows, :] + weights * (in_dot - disp_dot)).astype(BF16)
        grad_copy(c).start()

    each_chunk(in_step)
    acc[...] = jnp.zeros((SLOTS, HALF), F32)

    def keys_step(c):
        rows = rows_at(c)
        grad_copy(c).wait_recv()
        low = (lgs[rows, :].astype(F32) + lgr[rows, :].astype(F32)).astype(BF16)
        lg[rows, :] = low
        acc[...] += dot_tn(low, x[rows, :])

    each_chunk(keys_step)

    for h in range(2):
        for q in range(GROUPS6):
            turned = acc[h * 128:(h + 1) * 128, q * 128:(q + 1) * 128].T
            flat[h * HALF + q * 128:h * HALF + (q + 1) * 128, :] = turned
    kgmsg[...] = flat[0:2 * HALF, :].reshape(NT, KROWS, 128).astype(BF16)

    def key_target(i):
        b, c, a, d = i // 16, lax.rem(i // 4, 4), lax.rem(i // 2, 2), lax.rem(i, 2)
        px, py, pz = lax.rem(cx + a, 2), lax.rem(cy + 6 - b, 4), lax.rem(cz + 6 - c, 4)
        return px * 16 + py * 4 + pz, lax.rem(g + d, 2)

    def grad_send(i):
        p, d = key_target(i)
        return pltpu.make_async_remote_copy(
            kgmsg.at[d * 32 + p], kgland.at[t], a2a_s.at[5], a2a_r.at[5],
            device_id={"tok": g * 32 + p, "grp": d}, device_id_type=MESH,
        )

    def send_grad(i, _):
        grad_send(i).start()
        return 0

    def send_near(i, _):
        p, d = key_target(i)

        @pl.when((g * 32 + p != t) | (d != g))
        def _():
            grad_send(i).start()

        return 0

    lax.fori_loop(0, 40, send_grad, 0, unroll=True)
    lax.fori_loop(44, NT, send_grad, 0, unroll=True)
    lax.fori_loop(40, 44, send_near, 0)

    @pl.when(half == g)
    def _():
        pltpu.make_async_copy(kgmsg.at[g * 32 + lax.rem(t, 32)], kgland.at[t], a2a_r.at[5]).start()

    def tok_step(c):
        rows = rows_at(c)
        value = dot_nn(dispw[rows, :], rval[...]) + dot_nt(lg[rows, :], keyf[...])
        tok_out[rows, :] = value.astype(BF16)

    each_chunk(tok_step)

    landed(5, kgland)
    turned = jnp.sum(kgland[...].astype(F32), axis=0)
    parts = []
    for _ in range(3):
        parts.append(turned.astype(BF16))
        turned = turned - parts[-1].astype(F32)
    key_out[...] = dot_nt(parts[0], order) + (dot_nt(parts[1], order) + dot_nt(parts[2], order))

    for pair in (osg_pair, out_pair):
        pair.wait_send()

    for c in range(NCHUNK):
        logit_copy(c, 0).wait_send()
        logit_copy(c, 1).wait_send()
        grad_copy(c).wait_send()
    sent(1, osgmsg.at[pl.ds(0, NT - 1)])
    sent(2, slotland.at[0])
    sent(2, slotland.at[1, pl.ds(0, NT - 1)])
    sent(3, outland.at[pl.ds(0, NT - 1)])
    sent(4, rtland.at[0])
    sent(4, rtland.at[1, pl.ds(0, NT - 1)])

    @pl.when(half == g)
    def _():
        sent(0, keyland.at[pl.ds(0, NT - 1)])
        sent(5, kgmsg.at[pl.ds(0, NT - 1)])

    @pl.when(half != g)
    def _():
        sent(0, keyland)
        sent(5, kgmsg)


def store(lay, tok, key, win, wout, lay_out, tok_out, key_out, win_out, wout_out, sems):
    pairs = [(key, key_out)]
    for i in range(PIECES):
        rows = pl.ds(i * (TOK // PIECES), TOK // PIECES)
        pairs += [(lay.at[rows], lay_out.at[rows]), (tok.at[rows], tok_out.at[rows])]
        rows = pl.ds(i * (WIDTH // PIECES), WIDTH // PIECES)
        pairs.append((win.at[0, 0, rows], win_out.at[0, 0, rows]))
        rows = pl.ds(i * (HID // PIECES), HID // PIECES)
        pairs.append((wout.at[0, 0, rows], wout_out.at[0, 0, rows]))
    copies = [pltpu.make_async_copy(src, dst, sems.at[i]) for i, (src, dst) in enumerate(pairs)]
    for copy in copies:
        copy.start()
    for copy in copies:
        copy.wait()


def body(tokens, slot_keys, w_in, w_out, out_grad):
    anywhere = pl.BlockSpec(memory_space=pl.ANY)
    vmem = pl.BlockSpec(memory_space=pltpu.VMEM)
    buf = pltpu.VMEM
    dma = pltpu.SemaphoreType.DMA
    paired = buf((2, NT, 16, 128), BF16)
    short = buf((NT, DATA_ROWS, 128), BF16)
    layer_out, tokens_grad, keys_grad, w_in_grad, w_out_grad = pl.pallas_call(
        kernel,
        out_shape=(
            pltpu.VMEM((TOK, HALF), BF16),
            pltpu.VMEM((TOK, HALF), BF16),
            pltpu.VMEM((KROWS, 128), F32),
            pltpu.VMEM(w_in.shape, BF16),
            pltpu.VMEM(w_out.shape, BF16),
        ),
        in_specs=[anywhere] * 5,
        out_specs=[vmem, vmem, vmem, vmem, vmem],
        scratch_shapes=[
            buf((TOK, HALF), BF16),
            buf((TOK, HALF), BF16),
            buf((WIDTH, HID), BF16),
            buf((HID, WIDTH), BF16),
            buf((HID, WIDTH), BF16),
            buf((WIDTH, HID), BF16),
            buf((TOK, SLOTS), F32),
            buf((TOK, SLOTS), F32),
            buf((TOK, SLOTS), F32),
            buf((TOK, SLOTS), BF16),
            buf((TOK, SLOTS), BF16),
            buf((TOK, SLOTS), BF16),
            buf((TOK, SLOTS), BF16),
            buf((TOK, SLOTS), BF16),
            buf((SLOTS, HALF), F32),
            buf((128, HALF), F32),
            buf((2 * NT * 16, 128), F32),
            buf((HALF, SLOTS), BF16),
            buf((KROWS, 128), BF16),
            buf((KROWS, 128), BF16),
            short,
            short,
            short,
            paired,
            paired,
            buf((DATA_ROWS, 128), BF16),
            short,
            buf((2, 16, 128), BF16),
            paired,
            short,
            short,
            buf((SLOTS, HALF), BF16),
            buf((SLOTS, HALF), BF16),
            buf((8, 128), F32),
            buf((8, 128), F32),
            buf((DATA_ROWS, 128), F32),
            buf((SLOTS, HALF), BF16),
            buf((2, 128, HALF), BF16),
            buf((2, 16, 128), F32),
            buf((2, 16, 128), F32),
            buf((2, 16, 128), F32),
            buf((2, 16, 128), F32),
            buf((16, 128), F32),
            buf((16, WIDTH), F32),
            buf((16, WIDTH), F32),
            dma((5,)),
            dma((4,)),
            dma((4,)),
            dma((4,)),
            dma((2, NCHUNK)),
            dma((2, NCHUNK)),
            dma((NCHUNK,)),
            dma((NCHUNK,)),
            dma((6,)),
            dma((6,)),
        ],
        compiler_params=pltpu.CompilerParams(
            collective_id=0, has_side_effects=True, vmem_limit_bytes=46 * 1024 * 1024
        ),
        name="moe",
    )(tokens, slot_keys, w_in, w_out, out_grad)
    results = (layer_out, tokens_grad, keys_grad, w_in_grad, w_out_grad)
    results = tuple(pltpu.with_memory_space_constraint(r, pltpu.VMEM) for r in results)
    return pl.pallas_call(
        store,
        out_shape=tuple(jax.ShapeDtypeStruct(r.shape, r.dtype) for r in results),
        in_specs=[vmem] * 5,
        out_specs=[anywhere] * 5,
        scratch_shapes=[dma((4 * PIECES + 1,))],
        compiler_params=pltpu.CompilerParams(has_side_effects=True, vmem_limit_bytes=1024 * 1024),
        name="store",
    )(*results)


def solution(mesh):
    placed = (
        P("tok", "grp"),
        P("tok", "grp"),
        P("grp", "tok", None, None),
        P("grp", "tok", None, None),
        P("tok", "grp"),
    )
    return jax.shard_map(
        body,
        mesh=mesh,
        in_specs=placed,
        out_specs=(
            P("tok", "grp"),
            P("tok", "grp"),
            P("tok", "grp"),
            P("grp", "tok", None, None),
            P("grp", "tok", None, None),
        ),
        check_vma=False,
    )
```

time: 90.8 us -> 66.8 us (0.74)
  local copies, waits for them, and re-layouts: 13.2 us -> 0 us
  Pallas kernels: 76.7 us -> 66.1 us
    unnamed x11 -> x0, local copies, waits for them, and re-layouts: 12.3 us -> none
    pallas_call x1 -> x2, Pallas kernels: 76.7 us -> 66.1 us  [the longest x1 61.4 us: body(): pl.pallas_call(kernel, out_shape=(pltpu.VMEM((TOK, HALF), BF16), pltpu.VM...]
where the time goes in v2:
time: 66.8 us; the launch traced here: 66.7 us
  Pallas kernels  66.1 us (99%)
    pallas_call x1, Pallas kernels, body(): pl.pallas_call(kernel, out_shape=(pltpu.VMEM((TOK, HALF), BF16), pltpu.VM...  61.4 us
    pallas_call x1, Pallas kernels, body(): pl.pallas_call(store, out_shape=tuple((jax.ShapeDtypeStruct(r.shape, r.dt...  4.72 us

profile of v2, /device:TPU:1, one launch (start us, length us, event | category | flops | bytes accessed | tf_op | source)
XLA Modules:
  0.0 66.7 jit_solution(16266325479490591925)
XLA Ops:
  0.6 61.4 %moe.1 = (bf16[2048,768]{1,0:T(8,128)(2,1)S(1)}, bf16[2048,768]{1,0:T(8,128)(2,1)S(1)}, f32[24,128]{1,0:T(8,128)S(1)}, bf16[1,1,1536,1024]{3,2,1,0:T(8,128)(2,1)S(1)}, bf16[1,1,1024,1536]{3,2,1,0:T(8,128)(2,1)S(1)}) custom-call(bf16[2048,768]{1,0:T(8,128)(2,1)} %tokens.1, bf16[24,128]{1,0:T(8,128)(2,1)} %keys.1, bf16[1,1,1536,1024]{3,2,1,0:T(8,128)(2,1)} %w_in.1, ...), custom_call_target="tpu_custom_call" | custom-call | tf_op jit(solution)/shard_map/moe/pallas_call | solution.py:544
  62.0 4.7 %store.1 = (bf16[2048,768]{1,0:T(8,128)(2,1)}, bf16[2048,768]{1,0:T(8,128)(2,1)}, f32[24,128]{1,0:T(8,128)}, bf16[1,1,1536,1024]{3,2,1,0:T(8,128)(2,1)}, bf16[1,1,1024,1536]{3,2,1,0:T(8,128)(2,1)}) custom-call(bf16[2048,768]{1,0:T(8,128)(2,1)S(1)} %get-tuple-element.10.lay, bf16[2048,768]{1,0:T(8,128)(2,1)S(1)} %get-tuple-element.11.tok, ...), custom_call_target="tpu_custom_call" | custom-call | tf_op jit(solution)/shard_map/store/pallas_call | solution.py:619

commit v3 on v2

--- a/solution.py
+++ b/solution.py
@@ -413,9 +413,9 @@
     lane_sum = jnp.concatenate([routed_rows(j, 14) for j in range(SLOT_ROWS)], axis=0)
     disp_dot = join_hi_lo(lane_sum).T[0:1, :]
 
-    def grad_copy(c):
+    def grad_copy(c, group):
         return pltpu.make_async_remote_copy(
-            lgs.at[rows_at(c)], lgr.at[rows_at(c)], gs.at[c], gr.at[c],
+            lgs.at[rows_at(c)], lgr.at[rows_at(c)], gs.at[group, c], gr.at[group, c],
             device_id={"tok": t, "grp": other}, device_id_type=MESH,
         )
 
@@ -425,54 +425,54 @@
         dispw[rows, :] = weights.astype(BF16)
         in_dot = dot_nt(x[rows, :], rval[...])
         lgs[rows, :] = (comb[rows, :] + weights * (in_dot - disp_dot)).astype(BF16)
-        grad_copy(c).start()
+        grad_copy(c, 0).start()
 
     each_chunk(in_step)
-    acc[...] = jnp.zeros((SLOTS, HALF), F32)
-
-    def keys_step(c):
-        rows = rows_at(c)
-        grad_copy(c).wait_recv()
-        low = (lgs[rows, :].astype(F32) + lgr[rows, :].astype(F32)).astype(BF16)
-        lg[rows, :] = low
-        acc[...] += dot_tn(low, x[rows, :])
-
-    each_chunk(keys_step)
-
-    for h in range(2):
+
+    def key_target(i):
+        b, c, a = i // 8, lax.rem(i // 2, 4), lax.rem(i, 2)
+        px, py, pz = lax.rem(cx + a, 2), lax.rem(cy + 6 - b, 4), lax.rem(cz + 6 - c, 4)
+        return px * 16 + py * 4 + pz
+
+    for group in range(2):
+        lanes = slice(128 * group, 128 * (group + 1))
+        acc2[...] = jnp.zeros((128, HALF), F32)
+
+        def keys_step(c):
+            rows = rows_at(c)
+            if group == 0:
+                grad_copy(c, 0).wait_recv()
+            low = (lgs[rows, lanes].astype(F32) + lgr[rows, lanes].astype(F32)).astype(BF16)
+            lg[rows, lanes] = low
+            acc2[...] += dot_tn(low, x[rows, :])
+
+        each_chunk(keys_step)
         for q in range(GROUPS6):
-            turned = acc[h * 128:(h + 1) * 128, q * 128:(q + 1) * 128].T
-            flat[h * HALF + q * 128:h * HALF + (q + 1) * 128, :] = turned
-    kgmsg[...] = flat[0:2 * HALF, :].reshape(NT, KROWS, 128).astype(BF16)
-
-    def key_target(i):
-        b, c, a, d = i // 16, lax.rem(i // 4, 4), lax.rem(i // 2, 2), lax.rem(i, 2)
-        px, py, pz = lax.rem(cx + a, 2), lax.rem(cy + 6 - b, 4), lax.rem(cz + 6 - c, 4)
-        return px * 16 + py * 4 + pz, lax.rem(g + d, 2)
-
-    def grad_send(i):
-        p, d = key_target(i)
-        return pltpu.make_async_remote_copy(
-            kgmsg.at[d * 32 + p], kgland.at[t], a2a_s.at[5], a2a_r.at[5],
-            device_id={"tok": g * 32 + p, "grp": d}, device_id_type=MESH,
-        )
-
-    def send_grad(i, _):
-        grad_send(i).start()
-        return 0
-
-    def send_near(i, _):
-        p, d = key_target(i)
-
-        @pl.when((g * 32 + p != t) | (d != g))
-        def _():
-            grad_send(i).start()
-
-        return 0
-
-    lax.fori_loop(0, 40, send_grad, 0, unroll=True)
-    lax.fori_loop(44, NT, send_grad, 0, unroll=True)
-    lax.fori_loop(40, 44, send_near, 0)
+            flat[q * 128:(q + 1) * 128, :] = acc2[:, q * 128:(q + 1) * 128].T
+        kgmsg[group * 32:(group + 1) * 32, :, :] = flat[0:HALF, :].reshape(32, KROWS, 128).astype(BF16)
+
+        def grad_send(p, group=group):
+            return pltpu.make_async_remote_copy(
+                kgmsg.at[group * 32 + p], kgland.at[t], a2a_s.at[5], a2a_r.at[5],
+                device_id={"tok": g * 32 + p, "grp": group}, device_id_type=MESH,
+            )
+
+        def send_grad(i, _):
+            grad_send(key_target(i)).start()
+            return 0
+
+        def send_near(i, _):
+            p = key_target(i)
+
+            @pl.when((g * 32 + p != t) | (g != group))
+            def _():
+                grad_send(p).start()
+
+            return 0
+
+        lax.fori_loop(0, 20, send_grad, 0, unroll=True)
+        lax.fori_loop(22, 32, send_grad, 0, unroll=True)
+        lax.fori_loop(20, 22, send_near, 0)
 
     @pl.when(half == g)
     def _():
@@ -499,7 +499,7 @@
     for c in range(NCHUNK):
         logit_copy(c, 0).wait_send()
         logit_copy(c, 1).wait_send()
-        grad_copy(c).wait_send()
+        grad_copy(c, 0).wait_send()
     sent(1, osgmsg.at[pl.ds(0, NT - 1)])
     sent(2, slotland.at[0])
     sent(2, slotland.at[1, pl.ds(0, NT - 1)])
@@ -604,8 +604,8 @@
             dma((4,)),
             dma((2, NCHUNK)),
             dma((2, NCHUNK)),
-            dma((NCHUNK,)),
-            dma((NCHUNK,)),
+            dma((2, NCHUNK)),
+            dma((2, NCHUNK)),
             dma((6,)),
             dma((6,)),
         ],

time: 66.8 us -> 66.2 us (level)
  no operation moved by 1% of the time
where the time goes in v3:
time: 66.2 us; the launch traced here: 66.1 us
  Pallas kernels  65.5 us (99%)
    pallas_call x1, Pallas kernels, body(): pl.pallas_call(kernel, out_shape=(pltpu.VMEM((TOK, HALF), BF16), pltpu.VM...  60.7 us
    pallas_call x1, Pallas kernels, body(): pl.pallas_call(store, out_shape=tuple((jax.ShapeDtypeStruct(r.shape, r.dt...  4.72 us

profile of v3, /device:TPU:1, one launch (start us, length us, event | category | flops | bytes accessed | tf_op | source)
XLA Modules:
  0.0 66.1 jit_solution(12814667854205240934)
XLA Ops:
  0.6 60.7 %moe.1 = (bf16[2048,768]{1,0:T(8,128)(2,1)S(1)}, bf16[2048,768]{1,0:T(8,128)(2,1)S(1)}, f32[24,128]{1,0:T(8,128)S(1)}, bf16[1,1,1536,1024]{3,2,1,0:T(8,128)(2,1)S(1)}, bf16[1,1,1024,1536]{3,2,1,0:T(8,128)(2,1)S(1)}) custom-call(bf16[2048,768]{1,0:T(8,128)(2,1)} %tokens.1, bf16[24,128]{1,0:T(8,128)(2,1)} %keys.1, bf16[1,1,1536,1024]{3,2,1,0:T(8,128)(2,1)} %w_in.1, ...), custom_call_target="tpu_custom_call" | custom-call | tf_op jit(solution)/shard_map/moe/pallas_call | solution.py:544
  61.4 4.7 %store.1 = (bf16[2048,768]{1,0:T(8,128)(2,1)}, bf16[2048,768]{1,0:T(8,128)(2,1)}, f32[24,128]{1,0:T(8,128)}, bf16[1,1,1536,1024]{3,2,1,0:T(8,128)(2,1)}, bf16[1,1,1024,1536]{3,2,1,0:T(8,128)(2,1)}) custom-call(bf16[2048,768]{1,0:T(8,128)(2,1)S(1)} %get-tuple-element.10.lay, bf16[2048,768]{1,0:T(8,128)(2,1)S(1)} %get-tuple-element.11.tok, ...), custom_call_target="tpu_custom_call" | custom-call | tf_op jit(solution)/shard_map/store/pallas_call | solution.py:619
